TPU v7x, 128 devices: a whole 4x4x4 slice. The times are simulated.
128 devices in a mesh: dp: 4 (over y_lo, core), row: 16 (over x, z), col: 2 (over y_hi).
Axes of the slice: x: 4, y: 4 (y_hi: 2, y_lo: 2; y = y_hi * 2 + y_lo), z: 4, core: 2. Of those that a mesh axis runs over, the one named last changes fastest.
Arguments:
- tokens: bfloat16 [8192, 2048], P(('dp', 'row'), 'col'), may hold values from -6 to 6
- w_heads: bfloat16 [2048, 3, 2048], P('col', None, 'row'), may hold values from -0.125 to 0.125
- query_scale: float32 [2048], P('row'), may hold values from 0.1 to 1.9
- key_scale: float32 [2048], P('row'), may hold values from 0.1 to 1.9
- w_merge: bfloat16 [2048, 2048], P('row', 'col'), may hold values from -0.125 to 0.125
- attend_scale: float32 [2048], P('col'), may hold values from 0.1 to 1.9
- w_gateup: bfloat16 [2048, 2, 8192], P('col', None, 'row'), may hold values from -0.125 to 0.125
- w_down: bfloat16 [8192, 2048], P('row', 'col'), may hold values from -0.0625 to 0.0625
- dense_scale: float32 [2048], P('col'), may hold values from 0.1 to 1.9
- cotangent: bfloat16 [8192, 2048], P(('dp', 'row'), 'col'), may hold values from -6 to 6
Outputs:
- output: bfloat16 [8192, 2048], P(('dp', 'row'), 'col')
- grad_tokens: bfloat16 [8192, 2048], P(('dp', 'row'), 'col')
- grad_heads: float32 [2048, 3, 2048], P('col', None, 'row')
- grad_merge: float32 [2048, 2048], P('row', 'col')
- grad_gateup: float32 [2048, 2, 8192], P('col', None, 'row')
- grad_down: float32 [8192, 2048], P('row', 'col')
- grad_query: float32 [2048], replicated
- grad_key: float32 [2048], replicated
- grad_attend: float32 [2048], replicated
- grad_dense: float32 [2048], replicated
All inputs are finite; a program needn't handle non-finite values.
Results may differ from a plain program's by a relative error of at most 0.028.
Values may be sent and summed in bfloat16 or wider, within the bound.
No kernel may reach another device: no remote copies, remote signals or barrier semaphores. Data moves between devices by JAX's collectives and lax.ppermute only.
A program may use at most 128 MiB of HBM per device.

v0:
```python
import jax
import jax.numpy as jnp
from jax import lax
from jax.sharding import PartitionSpec as P

D = 2048
HEAD_DIM = 128
SEQ_LEN = 1024


EPSILON = 1e-06
THETA = 500000.0
NEGATIVE = -1e30


def contract(left, right, left_dim, right_dim):
    return lax.dot_general(
        left, right, (((left_dim,), (right_dim,)), ((), ())), preferred_element_type=jnp.float32
    )


def row_major(whole, col_count, row_count):
    sub = whole.shape[0] // (col_count * row_count)
    view = whole.reshape((col_count, row_count, sub) + whole.shape[1:])
    return jnp.swapaxes(view, 0, 1).reshape(whole.shape)


def column_blocks(whole, row_count, col_count):
    sub = whole.shape[0] // (row_count * col_count)
    return whole.reshape((row_count, col_count, sub) + whole.shape[1:])


def gather_group(shard, row_count, col_count):
    whole = lax.all_gather(shard, "row", axis=0, tiled=True)
    return row_major(whole, col_count, row_count)


def gather_parts(shard):
    return lax.all_gather(shard, "col", axis=0, tiled=True)


def depth_total(term, rows):
    return lax.psum_scatter(
        term(jnp.int32(0), lax.axis_size("col") * rows), "col", scatter_dimension=0, tiled=True
    )


def token_total(term, rows):
    return lax.psum_scatter(
        term(jnp.int32(0), rows * lax.axis_size("row")).astype(jnp.bfloat16),
        "row",
        scatter_dimension=0,
        tiled=True,
    ).astype(jnp.float32)


def feature_sums(values):
    return lax.psum(values, "col")


def head_sums(first, second):
    return lax.psum((first, second), "row")


def sum_from_rows(whole, weight, form, row_count, col_count):
    view = column_blocks(whole, row_count, col_count)
    block = view.shape[0] * view.shape[2]

    def term(start, count):
        result = jnp.einsum(form, view, weight, preferred_element_type=jnp.float32)
        return result.reshape(count, result.shape[-1])

    return token_total(term, block)


def spread_rows(whole, weight, weight_dim, rows):

    def term(start, count):
        return contract(whole, weight, 1, weight_dim)

    return depth_total(term, rows)


def project_in(shard, weight, row_count, col_count):
    whole = gather_group(shard, row_count, col_count)
    result = spread_rows(whole, weight, 0, whole.shape[0] // row_count)
    return (result, whole)


def project_out(values, weight, row_count, col_count):
    whole = gather_parts(values)
    result = sum_from_rows(whole, weight, "rmsk,ko->mrso", row_count, col_count)
    return (result, whole)


def project_in_back(grad, kept, weight, row_count, col_count):
    whole = gather_parts(grad)
    grad_in = sum_from_rows(whole, weight, "rmsk,ok->mrso", row_count, col_count)
    grad_weight = contract(kept, whole, 0, 0)
    return (grad_in, grad_weight)


def project_out_back(grad, kept, weight, row_count, col_count):
    whole = gather_group(grad, row_count, col_count)
    grad_in = spread_rows(whole, weight, 1, whole.shape[0] // row_count)
    grad_weight = contract(kept, whole, 0, 0)
    return (grad_in, grad_weight)


def rope_tables(place):
    pairs = HEAD_DIM // 2
    freq = THETA ** (-(jnp.arange(pairs, dtype=jnp.float32) * (2.0 / HEAD_DIM)))
    angle = place.astype(jnp.float32)[:, None] * freq[None, :]
    cosine = jnp.concatenate([jnp.cos(angle), jnp.cos(angle)], axis=1)
    sine = jnp.concatenate([jnp.sin(angle), jnp.sin(angle)], axis=1)
    return (cosine[:, None, :], sine[:, None, :])


def rotate(values, cosine, sine):
    pairs = values.shape[-1] // 2
    turned = jnp.concatenate([-values[..., pairs:], values[..., :pairs]], axis=-1)
    return values * cosine + turned * sine


def rotate_back(grad, cosine, sine):
    pairs = grad.shape[-1] // 2
    scaled = grad * sine
    turned = jnp.concatenate([scaled[..., pairs:], -scaled[..., :pairs]], axis=-1)
    return grad * cosine + turned


def local(
    tokens,
    w_heads,
    query_scale,
    key_scale,
    w_merge,
    attend_scale,
    w_gateup,
    w_down,
    dense_scale,
    cotangent,
):
    row_count = lax.axis_size("col")
    col_count = lax.axis_size("row")
    row_index = lax.axis_index("col")
    col_index = lax.axis_index("row")
    local_tokens, feature_width = tokens.shape
    sub = local_tokens // row_count
    group = local_tokens * col_count
    query_rows = group // row_count
    head_width = w_heads.shape[2]
    heads_here = head_width // HEAD_DIM
    hidden_width = w_gateup.shape[2]
    heads_flat = w_heads.reshape(feature_width, 3 * head_width)
    gateup_flat = w_gateup.reshape(feature_width, 2 * hidden_width)
    projected, kept_tokens = project_in(tokens, heads_flat, row_count, col_count)
    projected = projected.reshape(query_rows, 3, head_width)
    query_raw = projected[:, 0]
    key_raw = projected[:, 1]
    value_raw = projected[:, 2]
    query_power, key_power = head_sums(
        jnp.sum(query_raw * query_raw, axis=1), jnp.sum(key_raw * key_raw, axis=1)
    )
    query_rate = lax.rsqrt(query_power / D + EPSILON)[:, None]
    key_rate = lax.rsqrt(key_power / D + EPSILON)[:, None]
    query_hat = query_raw * query_rate
    key_hat = key_raw * key_rate
    local_index = jnp.arange(query_rows, dtype=jnp.int32)
    query_place = local_index // sub * local_tokens + row_index * sub + local_index % sub
    key_index = jnp.arange(group, dtype=jnp.int32)
    key_place = (
        key_index // sub % col_count * local_tokens
        + key_index // (col_count * sub) * sub
        + key_index % sub
    )
    same_sequence = (query_place // SEQ_LEN)[:, None] == (key_place // SEQ_LEN)[None, :]
    allowed = same_sequence & ((key_place % SEQ_LEN)[None, :] <= (query_place % SEQ_LEN)[:, None])
    cosine, sine = rope_tables(query_place % SEQ_LEN)
    shape_heads = (query_rows, heads_here, HEAD_DIM)
    query_low = rotate((query_hat * query_scale).reshape(shape_heads), cosine, sine).astype(
        jnp.bfloat16
    )
    key_low = rotate((key_hat * key_scale).reshape(shape_heads), cosine, sine).astype(jnp.bfloat16)
    value_low = value_raw.astype(jnp.bfloat16)
    keys_all, values_all = (
        lax.all_gather(key_low.reshape(query_rows, head_width), "col", axis=0, tiled=True),
        lax.all_gather(value_low, "col", axis=0, tiled=True),
    )
    keys_all = keys_all.reshape(group, heads_here, HEAD_DIM)
    values_all = values_all.reshape(group, heads_here, HEAD_DIM)
    scale = HEAD_DIM ** (-0.5)

    def scores_of():
        raw = (
            jnp.einsum("qhd,khd->hqk", query_low, keys_all, preferred_element_type=jnp.float32)
            * scale
        )
        return jnp.where(allowed[None], raw, NEGATIVE)

    scores = scores_of()
    top = jnp.max(scores, axis=2, keepdims=True)
    shifted = jnp.exp(scores - top)
    total = jnp.sum(shifted, axis=2, keepdims=True)
    log_total = top + jnp.log(total)
    probs_low = (shifted / total).astype(jnp.bfloat16)
    mixed = jnp.einsum("hqk,khd->qhd", probs_low, values_all, preferred_element_type=jnp.float32)
    mixed_low = mixed.reshape(query_rows, head_width).astype(jnp.bfloat16)
    attended, kept_mixed = project_out(mixed_low, w_merge, row_count, col_count)
    attend_power = feature_sums(jnp.sum(attended * attended, axis=1))
    attend_rate = lax.rsqrt(attend_power / D + EPSILON)[:, None]
    attend_hat = attended * attend_rate
    hidden = tokens.astype(jnp.float32) + attend_hat * attend_scale
    gateup, kept_hidden = project_in(hidden.astype(jnp.bfloat16), gateup_flat, row_count, col_count)
    gate = gateup[:, :hidden_width]
    upper = gateup[:, hidden_width:]
    sigmoid = jax.nn.sigmoid(gate)
    activated = gate * sigmoid
    act_low = (activated * upper).astype(jnp.bfloat16)
    dense, kept_act = project_out(act_low, w_down, row_count, col_count)
    dense_power = feature_sums(jnp.sum(dense * dense, axis=1))
    dense_rate = lax.rsqrt(dense_power / D + EPSILON)[:, None]
    dense_hat = dense * dense_rate
    output = (hidden + dense_hat * dense_scale).astype(jnp.bfloat16)
    grad_out = cotangent.astype(jnp.float32)
    dense_scaled = grad_out * dense_scale
    dense_dot = feature_sums(jnp.sum(dense_scaled * dense_hat, axis=1))[:, None]
    dense_back_low = (dense_rate * (dense_scaled - dense_hat * (dense_dot / D))).astype(
        jnp.bfloat16
    )
    dense_part = jnp.sum(grad_out * dense_hat, axis=0)
    act_back, grad_down = project_out_back(dense_back_low, kept_act, w_down, row_count, col_count)
    gate_back = act_back * upper * sigmoid * (1.0 + gate * (1.0 - sigmoid))
    up_back = act_back * activated
    gateup_back_low = jnp.concatenate([gate_back, up_back], axis=1).astype(jnp.bfloat16)
    hidden_mixed, grad_gateup = project_in_back(
        gateup_back_low, kept_hidden, gateup_flat, row_count, col_count
    )
    hidden_back = grad_out + hidden_mixed
    attend_scaled = hidden_back * attend_scale
    attend_dot = feature_sums(jnp.sum(attend_scaled * attend_hat, axis=1))[:, None]
    attended_back_low = (attend_rate * (attend_scaled - attend_hat * (attend_dot / D))).astype(
        jnp.bfloat16
    )
    attend_part = jnp.sum(hidden_back * attend_hat, axis=0)
    mixed_back, grad_merge = project_out_back(
        attended_back_low, kept_mixed, w_merge, row_count, col_count
    )
    mixed_back_low = mixed_back.astype(jnp.bfloat16).reshape(shape_heads)
    probs = jnp.exp(scores_of() - log_total)
    probs_back = jnp.einsum(
        "qhd,khd->hqk", mixed_back_low, values_all, preferred_element_type=jnp.float32
    )
    row_dot = jnp.sum(probs_back * probs, axis=2, keepdims=True)
    scores_back_low = (probs * (probs_back - row_dot)).astype(jnp.bfloat16)
    query_turned = (
        jnp.einsum("hqk,khd->qhd", scores_back_low, keys_all, preferred_element_type=jnp.float32)
        * scale
    )
    key_part = (
        jnp.einsum("hqk,qhd->khd", scores_back_low, query_low, preferred_element_type=jnp.float32)
        * scale
    )
    value_part = jnp.einsum(
        "hqk,qhd->khd",
        probs.astype(jnp.bfloat16),
        mixed_back_low,
        preferred_element_type=jnp.float32,
    )
    key_turned, value_back = (
        lax.psum_scatter(
            key_part.reshape(group, head_width).astype(jnp.bfloat16),
            "col",
            scatter_dimension=0,
            tiled=True,
        ).astype(jnp.float32),
        lax.psum_scatter(
            value_part.reshape(group, head_width).astype(jnp.bfloat16),
            "col",
            scatter_dimension=0,
            tiled=True,
        ).astype(jnp.float32),
    )
    query_norm_back = rotate_back(query_turned, cosine, sine).reshape(query_rows, head_width)
    key_norm_back = rotate_back(key_turned.reshape(shape_heads), cosine, sine).reshape(
        query_rows, head_width
    )
    query_scaled = query_norm_back * query_scale
    key_scaled = key_norm_back * key_scale
    query_dot, key_dot = head_sums(
        jnp.sum(query_scaled * query_hat, axis=1), jnp.sum(key_scaled * key_hat, axis=1)
    )
    query_back = query_rate * (query_scaled - query_hat * (query_dot[:, None] / D))
    key_back = key_rate * (key_scaled - key_hat * (key_dot[:, None] / D))
    query_part = jnp.sum(query_norm_back * query_hat, axis=0)
    key_gain_part = jnp.sum(key_norm_back * key_hat, axis=0)
    projected_back_low = (
        jnp.stack([query_back, key_back, value_back], axis=1)
        .reshape(query_rows, 3 * head_width)
        .astype(jnp.bfloat16)
    )
    tokens_back, grad_heads = project_in_back(
        projected_back_low, kept_tokens, heads_flat, row_count, col_count
    )
    grad_tokens = (hidden_back + tokens_back).astype(jnp.bfloat16)
    grad_heads, grad_merge, grad_gateup, grad_down = (
        lax.psum(grad_heads.astype(jnp.bfloat16), "dp").astype(jnp.float32),
        lax.psum(grad_merge.astype(jnp.bfloat16), "dp").astype(jnp.float32),
        lax.psum(grad_gateup.astype(jnp.bfloat16), "dp").astype(jnp.float32),
        lax.psum(grad_down.astype(jnp.bfloat16), "dp").astype(jnp.float32),
    )
    blank = jnp.zeros((D,), jnp.float32)
    gains = jnp.stack(
        [
            lax.dynamic_update_slice_in_dim(blank, query_part, col_index * head_width, 0),
            lax.dynamic_update_slice_in_dim(blank, key_gain_part, col_index * head_width, 0),
            lax.dynamic_update_slice_in_dim(blank, attend_part, row_index * feature_width, 0),
            lax.dynamic_update_slice_in_dim(blank, dense_part, row_index * feature_width, 0),
        ]
    )
    gains = lax.psum(gains, ("dp", "row", "col"))
    return (
        output,
        grad_tokens,
        grad_heads.reshape(feature_width, 3, head_width),
        grad_merge,
        grad_gateup.reshape(feature_width, 2, hidden_width),
        grad_down,
        gains[0],
        gains[1],
        gains[2],
        gains[3],
    )


def solution(mesh):
    in_specs = (
        P(("dp", "row"), "col"),
        P("col", None, "row"),
        P("row"),
        P("row"),
        P("row", "col"),
        P("col"),
        P("col", None, "row"),
        P("row", "col"),
        P("col"),
        P(("dp", "row"), "col"),
    )
    out_specs = (
        P(("dp", "row"), "col"),
        P(("dp", "row"), "col"),
        P("col", None, "row"),
        P("row", "col"),
        P("col", None, "row"),
        P("row", "col"),
        P(),
        P(),
        P(),
        P(),
    )
    return jax.shard_map(local, mesh=mesh, in_specs=in_specs, out_specs=out_specs, check_vma=False)
```

profile of v0, /device:TPU:1, one launch (start us, length us, event | category | flops | bytes accessed | tf_op | source)
XLA Modules:
  0.0 1255.7 jit_solution(2332973590455944170)
XLA Ops:
  9.4 55.7 %all-gather.11.cloned.1.call-done = bf16[2048,1024]{1,0:T(8,128)(2,1)} async-done(((bf16[128,1024]{1,0:T(8,128)(2,1)}), bf16[2048,1024]{1,0:T(8,128)(2,1)}) %all-gather.11.cloned.1.call-update) | async-done | bytes 4194320 | tf_op jit(solution)/shard_map/all_gather | solution.py:34
  76.7 44.2 %reduce-scatter.11.cloned.1.call-done = f32[1024,384]{1,0:T(8,128)} async-done(((f32[2048,384]{1,0:T(8,128)}), f32[1024,384]{1,0:T(8,128)}) %reduce-scatter.11.cloned.1.call-update) | async-done | bytes 1572880 | tf_op jit(solution)/shard_map/reduce_scatter | solution.py:43
  122.9 9.3 all-gather
  132.2 33.8 %all-reduce.1 = (f32[1024]{0:T(1024)S(1)}, f32[1024]{0:T(1024)S(1)}) all-reduce(f32[1024]{0:T(1024)S(1)} %get-tuple-element.17, f32[1024]{0:T(1024)S(1)} %get-tuple-element.16), channel_id=1, replica_groups=mesh['dp'=4,'row'=16,'col'=2] {'row'}, use_global_device_ids=true, to_apply=%region_4.0 | all-reduce | flops 2048 | bytes 16384 | tf_op jit(solution)/shard_map/psum | solution.py:62
  167.3 7.4 all-gather.1
  183.0 7.9 all-gather.2
  196.8 81.1 %reduce-scatter.13.cloned.1.call-done = bf16[128,1024]{1,0:T(8,128)(2,1)} async-done(((bf16[2048,1024]{1,0:T(8,128)(2,1)}), bf16[128,1024]{1,0:T(8,128)(2,1)}) %reduce-scatter.13.cloned.1.call-update) | async-done | bytes 262160 | tf_op jit(solution)/shard_map/reduce_scatter | solution.py:49
  289.6 50.3 %all-gather.13.cloned.1.call-done = bf16[2048,1024]{1,0:T(8,128)(2,1)} async-done(((bf16[128,1024]{1,0:T(8,128)(2,1)}), bf16[2048,1024]{1,0:T(8,128)(2,1)}) %all-gather.13.cloned.1.call-update) | async-done | bytes 4194320 | tf_op jit(solution)/shard_map/all_gather | solution.py:34
  344.7 6.6 fusion.111
  351.4 103.0 %reduce-scatter.15.cloned.1.call-done = f32[1024,1024]{1,0:T(8,128)} async-done(((f32[2048,1024]{1,0:T(8,128)}), f32[1024,1024]{1,0:T(8,128)}) %reduce-scatter.15.cloned.1.call-update) | async-done | bytes 4194320 | tf_op jit(solution)/shard_map/reduce_scatter | solution.py:43
  458.3 36.7 %all-gather.15.cloned.1.call-done = bf16[2048,512]{1,0:T(8,128)(2,1)} async-done(((bf16[1024,512]{1,0:T(8,128)(2,1)}), bf16[2048,512]{1,0:T(8,128)(2,1)}) %all-gather.15.cloned.1.call-update) | async-done | bytes 2097168 | tf_op jit(solution)/shard_map/all_gather | solution.py:39
  501.5 75.7 %reduce-scatter.17.cloned.1.call-done = bf16[128,1024]{1,0:T(8,128)(2,1)} async-done(((bf16[2048,1024]{1,0:T(8,128)(2,1)}), bf16[128,1024]{1,0:T(8,128)(2,1)}) %reduce-scatter.17.cloned.1.call-update) | async-done | bytes 262160 | tf_op jit(solution)/shard_map/reduce_scatter | solution.py:49
  592.2 54.8 %all-gather.17.cloned.1.call-done = bf16[2048,1024]{1,0:T(8,128)(2,1)} async-done(((bf16[128,1024]{1,0:T(8,128)(2,1)}), bf16[2048,1024]{1,0:T(8,128)(2,1)}) %all-gather.17.cloned.1.call-update) | async-done | bytes 4194320 | tf_op jit(solution)/shard_map/all_gather | solution.py:34
  656.2 58.0 %reduce-scatter.19.cloned.1.call-done = f32[1024,512]{1,0:T(8,128)} async-done(((f32[2048,512]{1,0:T(8,128)}), f32[1024,512]{1,0:T(8,128)}) %reduce-scatter.19.cloned.1.call-update) | async-done | bytes 2097168 | tf_op jit(solution)/shard_map/reduce_scatter | solution.py:43
  724.4 55.9 %all-gather.19.cloned.1.call-done = bf16[2048,1024]{1,0:T(8,128)(2,1)} async-done(((bf16[1024,1024]{1,0:T(8,128)(2,1)}), bf16[2048,1024]{1,0:T(8,128)(2,1)}) %all-gather.19.cloned.1.call-update) | async-done | bytes 4194320 | tf_op jit(solution)/shard_map/all_gather | solution.py:39
  780.3 7.4 convert_bitcast_fusion.1
  790.2 75.6 %reduce-scatter.21.cloned.1.call-done = bf16[128,1024]{1,0:T(8,128)(2,1)} async-done(((bf16[2048,1024]{1,0:T(8,128)(2,1)}), bf16[128,1024]{1,0:T(8,128)(2,1)}) %reduce-scatter.21.cloned.1.call-update) | async-done | bytes 262160 | tf_op jit(solution)/shard_map/reduce_scatter | solution.py:49
  874.5 53.8 %all-gather.21.cloned.1.call-done = bf16[2048,1024]{1,0:T(8,128)(2,1)} async-done(((bf16[128,1024]{1,0:T(8,128)(2,1)}), bf16[2048,1024]{1,0:T(8,128)(2,1)}) %all-gather.21.cloned.1.call-update) | async-done | bytes 4194320 | tf_op jit(solution)/shard_map/all_gather | solution.py:34
  935.5 23.8 %reduce-scatter.23.cloned.1.call-done = f32[1024,128]{1,0:T(8,128)} async-done(((f32[2048,128]{1,0:T(8,128)}), f32[1024,128]{1,0:T(8,128)}) %reduce-scatter.23.cloned.1.call-update) | async-done | bytes 524304 | tf_op jit(solution)/shard_map/reduce_scatter | solution.py:43
  994.6 33.8 %all-reduce = (f32[1024]{0:T(1024)S(1)}, f32[1024]{0:T(1024)S(1)}) all-reduce(f32[1024]{0:T(1024)S(1)} %get-tuple-element.14, f32[1024]{0:T(1024)S(1)} %get-tuple-element.13), channel_id=1, replica_groups=mesh['dp'=4,'row'=16,'col'=2] {'row'}, use_global_device_ids=true, to_apply=%region_26.27 | all-reduce | flops 2048 | bytes 16384 | tf_op jit(solution)/shard_map/psum | solution.py:62
  1051.7 13.9 %all-gather.23.cloned.1.call-done = bf16[2048,384]{0,1:T(8,128)(2,1)} async-done(((bf16[1024,384]{0,1:T(8,128)(2,1)}), bf16[2048,384]{0,1:T(8,128)(2,1)}) %all-gather.23.cloned.1.call-update) | async-done | bytes 1572880 | tf_op jit(solution)/shard_map/all_gather | solution.py:39
  1081.5 65.3 %psum.103 = f32[4,2048]{1,0:T(4,128)S(1)} all-reduce(f32[4,2048]{1,0:T(4,128)S(1)} %pad_maximum_fusion.6), channel_id=1, replica_groups=mesh['dp'=4,'row'=16,'col'=2] {'dp','row','col'}, use_global_device_ids=true, to_apply=%region_37.38 | all-reduce | flops 8192 | bytes 65536 | tf_op jit(solution)/shard_map/psum | solution.py:321
  1147.4 19.3 %all-reduce.5.cloned.1.call-done = (bf16[1024,3,128]{2,0,1:T(8,128)(2,1)}, bf16[128,1024]{1,0:T(8,128)(2,1)}, bf16[1024,2,512]{2,1,0:T(2,128)(2,1)}, bf16[512,1024]{1,0:T(8,128)(2,1)}) async-done(((bf16[1024,3,128]{2,0,1:T(8,128)(2,1)}, bf16[128,1024]{1,0:T(8,128)(2,1)}, bf16[1024,2,512]{2,1,0:T(2,128)(2,1)}, bf16[512,1024]{1,0:T(8,128)(2,1)}), (bf16[1024,3,128]{2,0,1:T(8,128)(2,1)}, ...) | async-done | bytes 4194320 | tf_op jit(solution)/shard_map/psum | solution.py:307
  1177.4 69.1 %reduce-scatter.29.cloned.1.call-done = bf16[128,1024]{1,0:T(8,128)(2,1)} async-done(((bf16[2048,1024]{1,0:T(8,128)(2,1)}), bf16[128,1024]{1,0:T(8,128)(2,1)}) %reduce-scatter.29.cloned.1.call-update) | async-done | bytes 262160 | tf_op jit(solution)/shard_map/reduce_scatter | solution.py:49
  (199 shorter events, 197.8 us)
Async XLA Ops:
  7.2 487.8 %copy-start = (bf16[512,1024]{1,0:T(8,128)(2,1)S(1)}, bf16[512,1024]{1,0:T(8,128)(2,1)}, u32[]{:S(2)}) copy-start(bf16[512,1024]{1,0:T(8,128)(2,1)} %param.17) | copy-start | bytes 3145732
  7.2 57.9 %all-gather.11.cloned.1.call-start = ((), (), s32[]{:S(2)}) async-start(), calls=%async_computation.10 | async-start | bytes 4456448 | tf_op jit(solution)/shard_map/all_gather | solution.py:34
  7.9 113.0 %reduce-scatter.11.cloned.1.call-start = ((), (), s32[]{:S(2)}) async-start(), calls=%async_computation.11 | async-start | bytes 4718592 | tf_op jit(solution)/shard_map/reduce_scatter | solution.py:43
  73.7 92.4 %copy-start.33 = (f32[128]{0:T(128)S(1)}, f32[128]{0:T(128)}, u32[]{:S(2)}) copy-start(f32[128]{0:T(128)} %param.12) | copy-start | bytes 1540
  73.7 92.4 %copy-start.34 = (f32[128]{0:T(128)S(1)}, f32[128]{0:T(128)}, u32[]{:S(2)}) copy-start(f32[128]{0:T(128)} %param.13) | copy-start | bytes 1540
  73.8 204.1 %reduce-scatter.13.cloned.1.call-start = ((), (), s32[]{:S(2)}) async-start(), calls=%async_computation.12 | async-start | bytes 4456448 | tf_op jit(solution)/shard_map/reduce_scatter | solution.py:49
  196.7 87.6 %copy-start.15 = (bf16[128,1024]{1,0:T(8,128)(2,1)S(1)}, bf16[128,1024]{1,0:T(8,128)(2,1)}, u32[]{:S(2)}) copy-start(bf16[128,1024]{1,0:T(8,128)(2,1)} %param.10) | copy-start | bytes 786436
  196.7 87.6 %copy-start.31 = (f32[1024]{0:T(1024)S(1)}, f32[1024]{0:T(1024)}, u32[]{:S(2)}) copy-start(f32[1024]{0:T(1024)} %param.15) | copy-start | bytes 12292
  196.7 143.2 %all-gather.13.cloned.1.call-start = ((), (), s32[]{:S(2)}) async-start(), calls=%async_computation.13 | async-start | bytes 4456448 | tf_op jit(solution)/shard_map/all_gather | solution.py:34
  286.1 168.3 %reduce-scatter.15.cloned.1.call-start = ((), (), s32[]{:S(2)}) async-start(), calls=%async_computation.14 | async-start | bytes 12582912 | tf_op jit(solution)/shard_map/reduce_scatter | solution.py:43
  351.4 143.6 %all-gather.15.cloned.1.call-start = ((), (), s32[]{:S(2)}) async-start(), calls=%async_computation.15 | async-start | bytes 3145728 | tf_op jit(solution)/shard_map/all_gather | solution.py:39
  458.3 118.9 %reduce-scatter.17.cloned.1.call-start = ((), (), s32[]{:S(2)}) async-start(), calls=%async_computation.16 | async-start | bytes 4456448 | tf_op jit(solution)/shard_map/reduce_scatter | solution.py:49
  501.4 82.2 %copy-start.32 = (f32[1024]{0:T(1024)S(1)}, f32[1024]{0:T(1024)}, u32[]{:S(2)}) copy-start(f32[1024]{0:T(1024)} %param.18) | copy-start | bytes 12292
  501.4 145.6 %all-gather.17.cloned.1.call-start = ((), (), s32[]{:S(2)}) async-start(), calls=%async_computation.17 | async-start | bytes 4456448 | tf_op jit(solution)/shard_map/all_gather | solution.py:34
  592.0 122.2 %reduce-scatter.19.cloned.1.call-start = ((), (), s32[]{:S(2)}) async-start(), calls=%async_computation.18 | async-start | bytes 6291456 | tf_op jit(solution)/shard_map/reduce_scatter | solution.py:43
  656.1 124.2 %all-gather.19.cloned.1.call-start = ((), (), s32[]{:S(2)}) async-start(), calls=%async_computation.19 | async-start | bytes 6291456 | tf_op jit(solution)/shard_map/all_gather | solution.py:39
  719.9 145.9 %reduce-scatter.21.cloned.1.call-start = ((), (), s32[]{:S(2)}) async-start(), calls=%async_computation.20 | async-start | bytes 4456448 | tf_op jit(solution)/shard_map/reduce_scatter | solution.py:49
  790.2 138.1 %all-gather.21.cloned.1.call-start = ((), (), s32[]{:S(2)}) async-start(), calls=%async_computation.21 | async-start | bytes 4456448 | tf_op jit(solution)/shard_map/all_gather | solution.py:34
  874.4 84.9 %reduce-scatter.23.cloned.1.call-start = ((), (), s32[]{:S(2)}) async-start(), calls=%async_computation.22 | async-start | bytes 1572864 | tf_op jit(solution)/shard_map/reduce_scatter | solution.py:43
  935.2 55.9 %reduce-scatter.25.cloned.1.call-start = ((), (), s32[]{:S(2)}) async-start(), calls=%async_computation.23 | async-start | bytes 786432 | tf_op jit(solution)/shard_map/reduce_scatter | solution.py:271
  972.9 57.6 %reduce-scatter.27.cloned.1.call-start = ((), (), s32[]{:S(2)}) async-start(), calls=%async_computation.24 | async-start | bytes 786432 | tf_op jit(solution)/shard_map/reduce_scatter | solution.py:277
  984.5 81.2 %all-gather.23.cloned.1.call-start = ((), (), s32[]{:S(2)}) async-start(), calls=%async_computation.25 | async-start | bytes 2359296 | tf_op jit(solution)/shard_map/all_gather | solution.py:39
  1032.6 134.1 %all-reduce.5.cloned.1.call-start = ((), (), s32[]{:S(2)}) async-start(), calls=%async_computation.27 | async-start | bytes 8388608 | tf_op jit(solution)/shard_map/psum | solution.py:307
  1073.5 173.0 %reduce-scatter.29.cloned.1.call-start = ((), (), s32[]{:S(2)}) async-start(), calls=%async_computation.26 | async-start | bytes 4456448 | tf_op jit(solution)/shard_map/reduce_scatter | solution.py:49
  (30 other events, 731.3 us)
Sparse Core Ops, SparseCore 0:
  10.2 54.8 all-gather.10
  73.9 46.9 reduce-scatter.10
  196.9 80.9 reduce-scatter.12
  286.2 53.6 all-gather.12
  351.5 102.8 reduce-scatter.14
  458.4 36.5 all-gather.14
  501.5 75.6 reduce-scatter.16
  592.1 54.8 all-gather.16
  656.2 57.9 reduce-scatter.18
  720.0 60.1 all-gather.18
  790.3 75.4 reduce-scatter.20
  874.5 53.7 all-gather.20
  935.3 23.9 reduce-scatter.22
  973.1 18.0 reduce-scatter.24
  993.9 17.9 reduce-scatter.26
  1032.8 32.8 all-gather.22
  1073.6 93.0 all-reduce.4
  1169.9 76.5 reduce-scatter.28
where the time goes:
time: 1270 us; the launch traced here: 1260 us
  waiting for transfers between devices  878 us (69%)
  blocking collectives  179 us (14%)
  matrix products  77.5 us (6%)
  local copies, waits for them, and re-layouts  54 us (4%)
  other arithmetic  50.2 us (4%)
  between operations  15.3 us (1%)
    reduce_scatter x4, waiting for transfers between devices, token_total(): lax.psum_scatter(term(jnp.int32(0), rows * lax.axis_size('row')).astype(j...  302 us
    reduce_scatter x4, waiting for transfers between devices, depth_total(): lax.psum_scatter(term(jnp.int32(0), lax.axis_size('col') * rows), 'col',...  229 us
    all_gather x4, waiting for transfers between devices, gather_group(): whole = lax.all_gather(shard, 'row', axis=0, tiled=True)  215 us
    all_gather x3, waiting for transfers between devices, gather_parts(): return lax.all_gather(shard, 'col', axis=0, tiled=True)  106 us
    psum x2, blocking collectives, head_sums(): return lax.psum((first, second), 'row')  67.6 us
    psum x1, blocking collectives, local(): gains = lax.psum(gains, ('dp', 'row', 'col'))  65.3 us
    dot_general x8, matrix products, contract(): lax.dot_general(left, right, (((left_dim,), (right_dim,)), ((), ())), pre...  37.4 us
  transfers between devices with their start and end apart: 18, of which 17 were waited for; matrix products, arithmetic and copies ran while one was open for 5% of the time, Pallas kernels for 0%

commit v1 on v0

v1 whole, which is shorter than its diff:
```python
import itertools

import jax
import jax.numpy as jnp
from jax import lax
from jax.sharding import Mesh
from jax.sharding import PartitionSpec as P

D = 2048
HEAD_DIM = 128
SEQ_LEN = 1024
HALF = 1024
SUB = 64
EPSILON = 1e-06
THETA = 500000.0
NEGATIVE = -1e30

LOW = jnp.bfloat16
WIDE = jnp.float32

NAMES = ("yl", "core", "xh", "xl", "z", "yh")
SIZES = {"yl": 2, "core": 2, "xh": 2, "xl": 2, "z": 4, "yh": 2}


def contract(left, right, left_dim, right_dim):
    return lax.dot_general(
        left, right, (((left_dim,), (right_dim,)), ((), ())), preferred_element_type=WIDE
    )


def pairs_of(axes, target):
    sizes = [SIZES[name] for name in axes]

    def flat(place):
        index = 0
        for value, size in zip(place, sizes):
            index = index * size + value
        return index

    return [
        (flat(place), flat(target(*place)))
        for place in itertools.product(*[range(size) for size in sizes])
    ]


def move(value, axes, target):
    return lax.ppermute(value, axes, pairs_of(axes, target))


def to_core(value):
    return move(value, ("core",), lambda c: (1 - c,))


def to_sibling(value):
    return move(value, ("yl",), lambda a: (1 - a,))


def slice_near(value):
    return move(
        value,
        ("core", "xh", "xl"),
        lambda c, a, b: (c, 1 - a, 1 - b) if c == a else (1 - c, a, b),
    )


def give_near(value):
    return move(
        value,
        ("core", "xh", "xl"),
        lambda c, a, b: (1 - c, a, b) if c == a else (c, 1 - a, 1 - b),
    )


def slice_far(value):
    return move(
        value,
        ("yl", "core", "xh", "xl", "yh"),
        lambda l, c, a, b, h: (1 - l, c, a, b, 1 - h)
        if c == a
        else (1 - l, 1 - c, 1 - a, 1 - b, 1 - h),
    )


def beside(function, value, rides, work=()):
    value, arrays = lax.optimization_barrier((value, tuple(array for _, array in rides)))
    moved = tuple(ride(array) for (ride, _), array in zip(rides, arrays))
    return lax.optimization_barrier((function(value), moved, work))


def exchange(rows):
    return lax.all_to_all(rows, ("xl", "z"), 0, 0, tiled=True)


def gather_tokens(shard, function, rides=(), work=()):
    copies = jnp.broadcast_to(shard[None], (8,) + shard.shape).reshape(8 * SUB, shard.shape[1])
    own, moved, work = beside(exchange, copies, rides, work)
    first, other = lax.optimization_barrier((function(0, own), to_core(own)))
    return (own, other), (first, function(1, other)), moved, work


def scatter_tokens(function, rides=(), work=()):
    arrived = to_core(function(1).astype(LOW))
    own, arrived = lax.optimization_barrier((function(0).astype(LOW), arrived))
    arrived, moved, work = beside(exchange, add_low(own, arrived), rides, work)
    total = jnp.sum(arrived.reshape(8, SUB, arrived.shape[1]).astype(WIDE), axis=0)
    return total, moved, work


def by_core(first, second):
    own_first = lax.axis_index("core") == 0
    return jnp.where(own_first, first, second), jnp.where(own_first, second, first)


def group_copies(rows):
    copies = jnp.broadcast_to(rows[None], (16,) + rows.shape).reshape(-1, 128)
    arrived = lax.all_to_all(copies, ("core", "xl", "z"), 0, 0, tiled=True)
    return arrived.reshape((16,) + rows.shape)


def group_sums(own, other, more=None):
    whole = jnp.concatenate(by_core(own, other), axis=0).reshape(16, 128)
    if more is not None:
        whole = jnp.concatenate([whole, more], axis=0)
    arrived = group_copies(whole)
    total = jnp.sum(arrived[:, :16], axis=0).reshape(2, 2, 512)
    return by_core(total[0], total[1]), arrived[:, 16:]


def other_groups(rows):
    axes = ("yl", "xh", "yh")
    copies = jnp.broadcast_to(rows[None], (8,) + rows.shape).reshape(-1, 128)
    arrived = lax.all_to_all(copies, axes, 0, 0, tiled=True)
    return jnp.sum(arrived.reshape((8,) + rows.shape), axis=0)


def both(function, *pairs):
    return tuple(function(*items) for items in zip(*pairs))


def add_low(first, *others):
    total = first.astype(WIDE)
    for other in others:
        total = total + other.astype(WIDE)
    return total.astype(LOW)


def regroup(block):
    core = lax.axis_index("core")
    high = lax.axis_index("yh")
    lower, upper = block[:SUB], block[SUB:]
    parts = []
    for j in (0, 1):
        piece = jnp.where((high ^ j) == 0, lower, upper)
        parts.append(move(piece, ("core", "yh"), lambda c, h: (h ^ j, c)))
    same = core == high
    return jnp.concatenate(
        [jnp.where(same, parts[0], parts[1]), jnp.where(same, parts[1], parts[0])], axis=1
    )


def ungroup(block):
    core = lax.axis_index("core")
    high = lax.axis_index("yh")
    near, far = block[:, :HALF], block[:, HALF:]
    parts = []
    for j in (0, 1):
        piece = jnp.where((core ^ j) == high, near, far)
        parts.append(move(piece, ("core", "yh"), lambda c, h: (h, c ^ j)))
    first = high == 0
    return jnp.concatenate(
        [jnp.where(first, parts[0], parts[1]), jnp.where(first, parts[1], parts[0])], axis=0
    )


def half_of_both(arrived_near, arrived_far):
    part = arrived_near.astype(WIDE) + arrived_far.astype(WIDE)
    rows = part.shape[0] // 2
    core = lax.axis_index("core")
    lower, upper = part[:rows], part[rows:]
    keep = jnp.where(core == 0, lower, upper)
    give = jnp.where(core == 0, upper, lower).astype(LOW)
    return (keep + to_core(give).astype(WIDE)).astype(LOW)


def whole_of_half(half, arrived):
    core = lax.axis_index("core")
    half = add_low(half, arrived)
    other = to_core(half)
    return jnp.concatenate(
        [jnp.where(core == 0, half, other), jnp.where(core == 0, other, half)], axis=0
    ).astype(WIDE)


def rope_tables(place):
    pairs = HEAD_DIM // 2
    freq = THETA ** (-(jnp.arange(pairs, dtype=WIDE) * (2.0 / HEAD_DIM)))
    angle = place.astype(WIDE)[:, None] * freq[None, :]
    cosine = jnp.concatenate([jnp.cos(angle), jnp.cos(angle)], axis=1)
    sine = jnp.concatenate([jnp.sin(angle), jnp.sin(angle)], axis=1)
    return (cosine, sine)


def rotate(values, cosine, sine):
    pairs = HEAD_DIM // 2
    turned = jnp.concatenate([-values[:, pairs:], values[:, :pairs]], axis=1)
    return values * cosine + turned * sine


def rotate_back(grad, cosine, sine):
    pairs = HEAD_DIM // 2
    scaled = grad * sine
    turned = jnp.concatenate([scaled[:, pairs:], -scaled[:, :pairs]], axis=1)
    return grad * cosine + turned


def local(
    tokens,
    w_heads,
    query_scale,
    key_scale,
    w_merge,
    attend_scale,
    w_gateup,
    w_down,
    dense_scale,
    cotangent,
):
    core = lax.axis_index("core")
    xh = lax.axis_index("xh")
    xl = lax.axis_index("xl")
    z = lax.axis_index("z")
    high = lax.axis_index("yh")

    shard = regroup(tokens)
    heads_in = w_heads.reshape(HALF, 3 * HEAD_DIM)
    gateup_in = lax.optimization_barrier(w_gateup.reshape(HALF, 2 * 512))
    head_scales = slice_near(jnp.stack([query_scale, key_scale]))
    query_scale, key_scale = head_scales[0], head_scales[1]
    width_scales = jnp.stack([attend_scale, dense_scale])
    width_scales = jnp.concatenate(
        [
            width_scales,
            move(width_scales, ("yl", "yh"), lambda l, h: (1 - l, 1 - h)),
        ],
        axis=1,
    )
    attend_scale, dense_scale = width_scales[0], width_scales[1]
    grad_out = regroup(cotangent)

    index = jnp.arange(512, dtype=jnp.int32)
    place = index // SUB * 128 + index % SUB
    places = (place + core * SUB, place + (1 - core) * SUB)
    key_place = jnp.concatenate(places)
    tables = both(rope_tables, places)
    scale = HEAD_DIM ** (-0.5)

    copies = jnp.broadcast_to(shard[None], (8,) + shard.shape).reshape(8 * SUB, D)
    own, moved, (tables, grad_out, gateup_in) = beside(
        exchange,
        copies,
        (
            (slice_near, heads_in),
            (slice_far, heads_in),
            (slice_near, w_merge),
            (slice_far, w_merge),
        ),
        (tables, grad_out, gateup_in),
    )
    grad_out = grad_out.astype(WIDE)
    heads = jnp.concatenate(moved[:2], axis=0)
    merge = jnp.concatenate(moved[2:], axis=1)

    def squares(query, key):
        return jnp.stack([jnp.sum(query * query, axis=1), jnp.sum(key * key, axis=1)])

    def attend_whole(own):
        first, other = lax.optimization_barrier((contract(own, heads, 1, 0), to_core(own)))
        projected = (first, contract(other, heads, 1, 0))
        query_raw = both(lambda rows: rows[:, :HEAD_DIM], projected)
        key_raw = both(lambda rows: rows[:, HEAD_DIM : 2 * HEAD_DIM], projected)
        value_low = jnp.concatenate(
            both(lambda rows: rows[:, 2 * HEAD_DIM :].astype(LOW), projected), axis=0
        )
        powers, _ = group_sums(*both(squares, query_raw, key_raw))
        rates = both(lambda rows: lax.rsqrt(rows / D + EPSILON), powers)
        query_rate = both(lambda rows: rows[0][:, None], rates)
        key_rate = both(lambda rows: rows[1][:, None], rates)
        query_hat = both(lambda raw, rate: raw * rate, query_raw, query_rate)
        key_hat = both(lambda raw, rate: raw * rate, key_raw, key_rate)
        query_low = both(
            lambda hat, table: rotate(hat * query_scale, *table).astype(LOW), query_hat, tables
        )
        key_low = jnp.concatenate(
            both(lambda hat, table: rotate(hat * key_scale, *table).astype(LOW), key_hat, tables),
            axis=0,
        )

        def attend(query, place):
            scores = scores_of(query, key_low, place)
            top = jnp.max(scores, axis=1, keepdims=True)
            shifted = jnp.exp(scores - top)
            total = jnp.sum(shifted, axis=1, keepdims=True)
            probs_low = (shifted / total).astype(LOW)
            mixed = contract(probs_low, value_low, 1, 0).astype(LOW)
            return mixed, top + jnp.log(total)

        attention = both(attend, query_low, places)
        mixed_low = both(lambda pair: pair[0], attention)
        log_total = both(lambda pair: pair[1], attention)
        return (
            (own, other),
            (query_rate, key_rate, query_hat, key_hat),
            (query_low, key_low, value_low),
            mixed_low,
            log_total,
        )

    def scores_of(query, key_low, place):
        allowed = key_place[None, :] <= place[:, None]
        return jnp.where(allowed, contract(query, key_low, 1, 1) * scale, NEGATIVE)

    (whole, norms, lows, mixed_low, log_total), gateup_parts, _ = beside(
        attend_whole, own, ((slice_near, gateup_in), (slice_far, gateup_in))
    )
    query_rate, key_rate, query_hat, key_hat = norms
    query_low, key_low, value_low = lows
    gateup_w = jnp.concatenate(gateup_parts, axis=0)

    attended, down_parts, gateup_w = scatter_tokens(
        lambda i: contract(mixed_low[i], merge, 1, 0),
        ((slice_near, w_down), (slice_far, w_down)),
        gateup_w,
    )
    attend_rate = lax.rsqrt(jnp.mean(attended * attended, axis=1, keepdims=True) + EPSILON)
    attend_hat = attended * attend_rate
    hidden = shard.astype(WIDE) + attend_hat * attend_scale

    def feed(i, rows):
        gateup = contract(rows, gateup_w, 1, 0)
        gate, upper = gateup[:, :512], gateup[:, 512:]
        return gate, upper, (gate * jax.nn.sigmoid(gate) * upper).astype(LOW)

    hidden_whole, fed, _, down = gather_tokens(
        hidden.astype(LOW), feed, (), jnp.concatenate(down_parts, axis=1)
    )
    act_low = both(lambda parts: parts[2], fed)
    dense, _, _ = scatter_tokens(lambda i: contract(act_low[i], down, 1, 0))
    dense_rate = lax.rsqrt(jnp.mean(dense * dense, axis=1, keepdims=True) + EPSILON)
    dense_hat = dense * dense_rate
    output = (hidden + dense_hat * dense_scale).astype(LOW)

    dense_scaled = grad_out * dense_scale
    dense_dot = jnp.mean(dense_scaled * dense_hat, axis=1, keepdims=True)
    dense_back_low = (dense_rate * (dense_scaled - dense_hat * dense_dot)).astype(LOW)
    dense_part = jnp.sum(grad_out * dense_hat, axis=0)

    def back_through(i, rows):
        gate, upper, _ = fed[i]
        act_back = contract(rows, down, 1, 1)
        sigmoid = jax.nn.sigmoid(gate)
        gate_back = act_back * upper * sigmoid * (1.0 + gate * (1.0 - sigmoid))
        up_back = act_back * (gate * sigmoid)
        return jnp.concatenate([gate_back, up_back], axis=1).astype(LOW)

    dense_back, gateup_back_low, _, _ = gather_tokens(dense_back_low, back_through)

    def weight_grad(left, right):
        return (contract(left[0], right[0], 0, 0) + contract(left[1], right[1], 0, 0)).astype(LOW)

    grad_down = weight_grad(act_low, dense_back)
    hidden_back, down_parts, (grad_gateup, output) = scatter_tokens(
        lambda i: contract(gateup_back_low[i], gateup_w, 1, 1),
        ((give_near, grad_down[:, :HALF]), (slice_far, grad_down[:, HALF:])),
        (weight_grad(hidden_whole, gateup_back_low), ungroup(output)),
    )
    hidden_back = grad_out + hidden_back

    attend_scaled = hidden_back * attend_scale
    attend_dot = jnp.mean(attend_scaled * attend_hat, axis=1, keepdims=True)
    attended_back_low = (attend_rate * (attend_scaled - attend_hat * attend_dot)).astype(LOW)
    attend_part = jnp.sum(hidden_back * attend_hat, axis=0)

    attended_back, mixed_back_low, gateup_upper, _ = gather_tokens(
        attended_back_low,
        lambda i, rows: contract(rows, merge, 1, 1).astype(LOW),
        ((give_near, grad_gateup[:512]), (slice_far, grad_gateup[HALF : HALF + 512])),
    )
    grad_merge = weight_grad(mixed_low, attended_back)
    down_half = half_of_both(*down_parts)
    gateup_upper = half_of_both(*gateup_upper)

    def attend_back(query, place, log_total, mixed_back):
        probs = jnp.exp(scores_of(query, key_low, place) - log_total)
        probs_back = contract(mixed_back, value_low, 1, 1)
        row_dot = jnp.sum(probs_back * probs, axis=1, keepdims=True)
        scores_back = (probs * (probs_back - row_dot)).astype(LOW)
        query_turned = contract(scores_back, key_low, 1, 0) * scale
        return query_turned, scores_back, probs.astype(LOW)

    def products(query, query_hat, key, key_hat):
        return jnp.stack([jnp.sum(query * query_hat, axis=1), jnp.sum(key * key_hat, axis=1)])

    def through_norm(rate, scaled, hat, dot):
        return rate * (scaled - hat * dot[:, None])

    def column_sum(first, second):
        return sum(both(lambda a, b: jnp.sum(a * b, axis=0), first, second))

    def attend_whole_back(mixed_back_low):
        backs = both(attend_back, query_low, places, log_total, mixed_back_low)
        query_norm_back = both(lambda back, table: rotate_back(back[0], *table), backs, tables)
        scores_back = (backs[0][1], backs[1][1])
        probs_low = (backs[0][2], backs[1][2])
        key_turned = scale * (
            contract(scores_back[0], query_low[0], 0, 0)
            + contract(scores_back[1], query_low[1], 0, 0)
        )
        value_back = contract(probs_low[0], mixed_back_low[0], 0, 0) + contract(
            probs_low[1], mixed_back_low[1], 0, 0
        )
        value_back = (value_back[:512], value_back[512:])
        key_norm_back = both(
            lambda rows, table: rotate_back(rows, *table),
            (key_turned[:512], key_turned[512:]),
            tables,
        )
        query_scaled = both(lambda rows: rows * query_scale, query_norm_back)
        key_scaled = both(lambda rows: rows * key_scale, key_norm_back)
        parts = jnp.concatenate(
            [
                column_sum(query_norm_back, query_hat)[None],
                column_sum(key_norm_back, key_hat)[None],
                attend_part.reshape(16, 128),
                dense_part.reshape(16, 128),
            ],
            axis=0,
        )
        dots, parts = group_sums(
            *both(products, query_scaled, query_hat, key_scaled, key_hat), parts
        )
        query_back = both(
            through_norm, query_rate, query_scaled, query_hat, (dots[0][0] / D, dots[1][0] / D)
        )
        key_back = both(
            through_norm, key_rate, key_scaled, key_hat, (dots[0][1] / D, dots[1][1] / D)
        )
        back = both(
            lambda *parts: jnp.concatenate(parts, axis=1).astype(LOW),
            query_back,
            key_back,
            value_back,
        )
        return back, parts

    (projected_back_low, parts), moved, _ = beside(
        attend_whole_back,
        mixed_back_low,
        (
            (give_near, grad_gateup[512:HALF]),
            (slice_far, grad_gateup[HALF + 512 :]),
            (give_near, grad_merge[:, :HALF]),
            (slice_far, grad_merge[:, HALF:]),
            (to_sibling, down_half),
        ),
    )
    gateup_lower = half_of_both(*moved[:2])
    merge_half = half_of_both(*moved[2:4])
    grad_heads = weight_grad(whole, projected_back_low)

    rows = parts[:, :2].reshape(2, 2, 4, 2, 128)
    straight = (jnp.arange(2) == xh)[:, None, None, None, None]
    rows = jnp.where(straight, rows, rows[:, ::-1])
    rows = jnp.moveaxis(rows.reshape(16, 2, 128), 1, 0).reshape(32, 128)
    width = jnp.sum(parts[:, 2:], axis=0).reshape(2, 2, 8, 128)
    width = jnp.where(high == 0, width, width[:, ::-1]).reshape(32, 128)
    gains = jnp.concatenate([rows, width], axis=0)

    tokens_back, moved, grad_down = scatter_tokens(
        lambda i: contract(projected_back_low[i], heads, 1, 1),
        (
            (give_near, grad_heads[:HALF]),
            (slice_far, grad_heads[HALF:]),
            (to_sibling, gateup_upper),
            (to_sibling, gateup_lower),
            (to_sibling, merge_half),
            (other_groups, gains),
        ),
        whole_of_half(down_half, moved[4]),
    )
    grad_tokens = ungroup((hidden_back + tokens_back).astype(LOW))
    heads_half = half_of_both(*moved[:2])
    grad_heads = whole_of_half(heads_half, to_sibling(heads_half))
    grad_gateup = jnp.concatenate(
        [whole_of_half(gateup_upper, moved[2]), whole_of_half(gateup_lower, moved[3])], axis=0
    )
    grad_merge = whole_of_half(merge_half, moved[4])
    gains = moved[5].reshape(4, D)
    return (
        output,
        grad_tokens,
        grad_heads.reshape(HALF, 3, HEAD_DIM),
        grad_merge,
        grad_gateup.reshape(HALF, 2, 512),
        grad_down,
        gains[0],
        gains[1],
        gains[2],
        gains[3],
    )


def solution(mesh):
    fine = Mesh(mesh.devices.reshape(tuple(SIZES[name] for name in NAMES)), NAMES)
    dp, row, col = ("yl", "core"), ("xh", "xl", "z"), "yh"
    in_specs = (
        P(dp + row, col),
        P(col, None, row),
        P(row),
        P(row),
        P(row, col),
        P(col),
        P(col, None, row),
        P(row, col),
        P(col),
        P(dp + row, col),
    )
    out_specs = (
        P(dp + row, col),
        P(dp + row, col),
        P(col, None, row),
        P(row, col),
        P(col, None, row),
        P(row, col),
        P(),
        P(),
        P(),
        P(),
    )
    return jax.shard_map(local, mesh=fine, in_specs=in_specs, out_specs=out_specs, check_vma=False)
```

time: 1270 us -> 554 us (0.44)
  waiting for transfers between devices: 878 us -> 175 us
  starting transfers between devices: 1.38 us -> 121 us
  blocking collectives: 179 us -> 70.6 us
  other arithmetic: 50.2 us -> 71.4 us
  matrix products: 77.5 us -> 61.7 us
    reduce_scatter x10 -> x0, waiting for transfers between devices: 537 us -> none  [the longest x4 302 us: token_total(): lax.psum_scatter(term(jnp.int32(0), rows * lax.axis_size('row')).astype(j...]
    all_gather x7 -> x0, waiting for transfers between devices: 321 us -> none  [the longest x4 215 us: gather_group(): whole = lax.all_gather(shard, 'row', axis=0, tiled=True)]
    ppermute x0 -> x51, waiting for transfers between devices: none -> 154 us  [move(): return lax.ppermute(value, axes, pairs_of(axes, target))]
    psum x7 -> x0, blocking collectives: 154 us -> none  [the longest x2 67.6 us: head_sums(): return lax.psum((first, second), 'row')]
    ppermute x0 -> x51, starting transfers between devices: none -> 82.5 us  [move(): return lax.ppermute(value, axes, pairs_of(axes, target))]
    all_to_all x0 -> x3, blocking collectives: none -> 70.6 us  [the longest x2 58.4 us: exchange(): return lax.all_to_all(rows, ('xl', 'z'), 0, 0, tiled=True)]
    dot_general x10 -> x0, matrix products: 40.1 us -> none  [the longest x4 17.4 us: term(): result = jnp.einsum(form, view, weight, preferred_element_type=jnp.float32)]
    all_to_all x0 -> x8, starting transfers between devices: none -> 38.6 us  [the longest x6 28.3 us: exchange(): return lax.all_to_all(rows, ('xl', 'z'), 0, 0, tiled=True)]
  transfers between devices with their start and end apart: 18 -> 59, of which waited for: 17 -> 25; matrix products, arithmetic and copies ran while one was open for 5% -> 20% of each run, Pallas kernels for 0% -> 0%
where the time goes in v1:
time: 554 us; the launch traced here: 545 us
  waiting for transfers between devices  175 us (32%)
  starting transfers between devices  121 us (22%)
  other arithmetic  71.4 us (13%)
  blocking collectives  70.6 us (13%)
  matrix products  61.7 us (11%)
  local copies, waits for them, and re-layouts  42.7 us (8%)
    ppermute x51, waiting for transfers between devices, move(): return lax.ppermute(value, axes, pairs_of(axes, target))  154 us
    ppermute x51, starting transfers between devices, move(): return lax.ppermute(value, axes, pairs_of(axes, target))  82.5 us
    dot_general x38, matrix products, contract(): lax.dot_general(left, right, (((left_dim,), (right_dim,)), ((), ())), pre...  61.7 us
    all_to_all x2, blocking collectives, exchange(): return lax.all_to_all(rows, ('xl', 'z'), 0, 0, tiled=True)  58.4 us
    all_to_all x6, starting transfers between devices, exchange(): return lax.all_to_all(rows, ('xl', 'z'), 0, 0, tiled=True)  28.3 us
    unnamed x185, local copies, waits for them, and re-layouts  22 us
    all_to_all x6, waiting for transfers between devices, exchange(): return lax.all_to_all(rows, ('xl', 'z'), 0, 0, tiled=True)  16.5 us
    convert_element_type x9, other arithmetic, add_low(): return total.astype(LOW)  14.7 us
  transfers between devices with their start and end apart: 59, of which 25 were waited for; matrix products, arithmetic and copies ran while one was open for 20% of the time, Pallas kernels for 0%

profile of v1, /device:TPU:1, one launch (start us, length us, event | category | flops | bytes accessed | tf_op | source)
XLA Modules:
  0.0 545.5 jit_solution(15243084925437018737)
XLA Ops:
  1.6 6.2 %collective-permute-start = (bf16[64,1024]{1,0:T(8,128)(2,1)S(1)}, bf16[64,1024]{1,0:T(8,128)(2,1)S(1)}, u32[]{:S(2)}, u32[]{:S(2)}) collective-permute-start(bf16[64,1024]{1,0:T(8,128)(2,1)S(1)} %get-tuple-element.368), channel_id=1, source_target_pairs={{0,0},{1,32},{32,1},{33,33},{2,2},{3,34},{34,3},{35,35},{4,4},{5,3... | collective-permute-start | bytes 393224 | tf_op jit(solution)/shard_map/ppermute | solution.py:47
  13.4 6.1 %all-to-all-start = ((bf16[8,64,2048]{2,1,0:T(8,128)(2,1)}), bf16[8,64,2048]{2,1,0:T(8,128)(2,1)S(1)}, u32[]{:S(2)}, u32[]{:S(2)}) async-start(bf16[8,64,2048]{2,1,0:T(8,128)(2,1)} %broadcast_in_dim.28), calls=%async_computation | async-start | bytes 4194304 | tf_op jit(solution)/shard_map/all_to_all | solution.py:91
  19.6 4.8 collective-permute-start.6
  36.2 16.8 %collective-permute-done.4 = bf16[128,1024]{1,0:T(8,128)(2,1)S(1)} collective-permute-done((bf16[128,1024]{1,0:T(8,128)(2,1)S(1)}, bf16[128,1024]{1,0:T(8,128)(2,1)S(1)}, u32[]{:S(2)}, u32[]{:S(2)}) %collective-permute-start.4) | collective-permute-done | bytes 262176 | tf_op jit(solution)/shard_map/ppermute | solution.py:47
  75.9 5.5 %all-to-all-start.1 = ((f32[16,16,128]{2,1,0:T(8,128)}), f32[16,16,128]{2,1,0:T(8,128)S(1)}, u32[]{:S(2)}, u32[]{:S(2)}) async-start(f32[16,16,128]{2,1,0:T(8,128)} %broadcast_in_dim.30), calls=%async_computation.1 | async-start | bytes 262144 | tf_op jit(solution)/shard_map/all_to_all | solution.py:116
  96.9 14.5 %collective-permute-done.10 = bf16[1024,1024]{1,0:T(8,128)(2,1)} collective-permute-done((bf16[1024,1024]{1,0:T(8,128)(2,1)}, bf16[1024,1024]{1,0:T(8,128)(2,1)}, u32[]{:S(2)}, u32[]{:S(2)}) %collective-permute-start.10) | collective-permute-done | bytes 2097184 | tf_op jit(solution)/shard_map/ppermute | solution.py:47
  134.5 4.7 pad_maximum_fusion
  139.2 11.5 %collective-permute-done.13 = bf16[512,1024]{1,0:T(8,128)(2,1)S(1)} collective-permute-done((bf16[512,1024]{1,0:T(8,128)(2,1)}, bf16[512,1024]{1,0:T(8,128)(2,1)S(1)}, u32[]{:S(2)}, u32[]{:S(2)}) %collective-permute-start.13) | collective-permute-done | bytes 1048608 | tf_op jit(solution)/shard_map/ppermute | solution.py:47
  164.6 16.5 %all-to-all-done.3 = bf16[8,64,2048]{2,1,0:T(8,128)(2,1)S(1)} async-done(((bf16[8,64,2048]{2,1,0:T(8,128)(2,1)}), bf16[8,64,2048]{2,1,0:T(8,128)(2,1)S(1)}, u32[]{:S(2)}, u32[]{:S(2)}) %all-to-all-start.3) | async-done | bytes 2097184 | tf_op jit(solution)/shard_map/all_to_all | solution.py:91
  181.1 8.0 %collective-permute-start.16 = (bf16[512,2048]{1,0:T(8,128)(2,1)S(1)}, bf16[512,2048]{1,0:T(8,128)(2,1)S(1)}, u32[]{:S(2)}, u32[]{:S(2)}) collective-permute-start(bf16[512,2048]{1,0:T(8,128)(2,1)S(1)} %bitcast.177), channel_id=1, source_target_pairs={{0,32},{32,0},{1,33},{33,1},{2,34},{34,2},{3,35},{35,3},{4,36},{36... | collective-permute-start | bytes 6291464 | tf_op jit(solution)/shard_map/ppermute | solution.py:47
  207.2 28.8 %all_to_all.114 = bf16[8,64,2048]{2,1,0:T(8,128)(2,1)S(1)} all-to-all(bf16[8,64,2048]{2,1,0:T(8,128)(2,1)S(1)} %bitcast.170), channel_id=1, replica_groups=mesh['yl'=2,'core'=2,'xh'=2,'xl'=2,'z'=4,'yh'=2] {'xl','z'}, dimensions={0} | all-to-all | bytes 4194304 | tf_op jit(solution)/shard_map/all_to_all | solution.py:91
  238.8 29.7 %all_to_all.115 = bf16[8,64,2048]{2,1,0:T(8,128)(2,1)S(1)} all-to-all(bf16[8,64,2048]{2,1,0:T(8,128)(2,1)S(1)} %broadcast_in_dim.33), channel_id=1, replica_groups=mesh['yl'=2,'core'=2,'xh'=2,'xl'=2,'z'=4,'yh'=2] {'xl','z'}, dimensions={0} | all-to-all | bytes 4194304 | tf_op jit(solution)/shard_map/all_to_all | solution.py:91
  300.7 7.0 %collective-permute-done.22 = bf16[64,1024]{1,0:T(8,128)(2,1)S(1)} collective-permute-done((bf16[64,1024]{1,0:T(8,128)(2,1)S(1)}, bf16[64,1024]{1,0:T(8,128)(2,1)S(1)}, u32[]{:S(2)}, u32[]{:S(2)}) %collective-permute-start.22) | collective-permute-done | bytes 131104 | tf_op jit(solution)/shard_map/ppermute | solution.py:47
  308.5 5.4 collective-permute-start.20
  320.1 4.6 add_convert_fusion
  326.9 12.8 %collective-permute-done.21 = bf16[512,1024]{1,0:T(8,128)(2,1)} collective-permute-done((bf16[512,1024]{1,0:T(8,128)(2,1)}, bf16[512,1024]{1,0:T(8,128)(2,1)}, u32[]{:S(2)}, u32[]{:S(2)}) %collective-permute-start.21) | collective-permute-done | bytes 1048608 | tf_op jit(solution)/shard_map/ppermute | solution.py:47
  357.2 6.5 %collective-permute-done.24 = bf16[512,1024]{1,0:T(8,128)(2,1)S(1)} collective-permute-done((bf16[512,1024]{1,0:T(8,128)(2,1)}, bf16[512,1024]{1,0:T(8,128)(2,1)S(1)}, u32[]{:S(2)}, u32[]{:S(2)}) %collective-permute-start.24) | collective-permute-done | bytes 1048608 | tf_op jit(solution)/shard_map/ppermute | solution.py:47
  363.7 15.0 %collective-permute-done.25 = bf16[512,1024]{1,0:T(8,128)(2,1)S(1)} collective-permute-done((bf16[512,1024]{1,0:T(8,128)(2,1)}, bf16[512,1024]{1,0:T(8,128)(2,1)S(1)}, u32[]{:S(2)}, u32[]{:S(2)}) %collective-permute-start.25) | collective-permute-done | bytes 1048608 | tf_op jit(solution)/shard_map/ppermute | solution.py:47
  405.8 4.8 all-to-all-start.8
  426.0 15.5 %collective-permute-done.30 = bf16[128,1024]{1,0:T(8,128)(2,1)} collective-permute-done((bf16[128,1024]{1,0:T(8,128)(2,1)}, bf16[128,1024]{1,0:T(8,128)(2,1)}, u32[]{:S(2)}, u32[]{:S(2)}) %collective-permute-start.30) | collective-permute-done | bytes 262176 | tf_op jit(solution)/shard_map/ppermute | solution.py:47
  461.2 12.2 %all_to_all.116 = f32[8,64,128]{2,1,0:T(8,128)} all-to-all(f32[8,64,128]{2,1,0:T(8,128)S(1)} %broadcast_in_dim.37), channel_id=1, replica_groups=mesh['yl'=2,'core'=2,'xh'=2,'xl'=2,'z'=4,'yh'=2] {'yl','xh','yh'}, dimensions={0} | all-to-all | bytes 524288 | tf_op jit(solution)/shard_map/all_to_all | solution.py:132
  473.4 5.8 %all-to-all-start.9 = ((bf16[8,64,2048]{2,1,0:T(8,128)(2,1)}), bf16[8,64,2048]{2,1,0:T(8,128)(2,1)S(1)}, u32[]{:S(2)}, u32[]{:S(2)}) async-start(bf16[8,64,2048]{2,1,0:T(8,128)(2,1)} %bitcast.68), calls=%async_computation.9 | async-start | bytes 4194304 | tf_op jit(solution)/shard_map/all_to_all | solution.py:91
  490.0 21.4 %collective-permute-done.41 = bf16[64,1024]{1,0:T(8,128)(2,1)} collective-permute-done((bf16[64,1024]{1,0:T(8,128)(2,1)S(1)}, bf16[64,1024]{1,0:T(8,128)(2,1)}, u32[]{:S(2)}, u32[]{:S(2)}) %collective-permute-start.41) | collective-permute-done | bytes 131104 | tf_op jit(solution)/shard_map/ppermute | solution.py:47
  528.1 8.5 %collective-permute-done.46 = bf16[512,384]{1,0:T(8,128)(2,1)} collective-permute-done((bf16[512,384]{1,0:T(8,128)(2,1)S(1)}, bf16[512,384]{1,0:T(8,128)(2,1)}, u32[]{:S(2)}, u32[]{:S(2)}) %collective-permute-start.46) | collective-permute-done | bytes 393248 | tf_op jit(solution)/shard_map/ppermute | solution.py:47
  (476 shorter events, 270.4 us)
Async XLA Ops:
  13.4 41.9 %all-to-all-start = ((bf16[8,64,2048]{2,1,0:T(8,128)(2,1)}), bf16[8,64,2048]{2,1,0:T(8,128)(2,1)S(1)}, u32[]{:S(2)}, u32[]{:S(2)}) async-start(bf16[8,64,2048]{2,1,0:T(8,128)(2,1)} %broadcast_in_dim.28), calls=%async_computation | async-start | bytes 4194304 | tf_op jit(solution)/shard_map/all_to_all | solution.py:91
  27.3 27.1 %collective-permute-start.2 = (bf16[1024,384]{0,1:T(8,128)(2,1)}, bf16[1024,384]{0,1:T(8,128)(2,1)S(1)}, u32[]{:S(2)}, u32[]{:S(2)}) collective-permute-start(bf16[1024,384]{0,1:T(8,128)(2,1)} %bitcast.1), channel_id=1, source_target_pairs={{0,24},{8,16},{16,48},{24,56},{32,0},{40,8},{48,40},{56,32},{1,25}... | collective-permute-start | bytes 2359304 | tf_op jit(solution)/shard_map/ppermute | solution.py:47
  27.7 27.6 %collective-permute-start.3 = (bf16[1024,384]{0,1:T(8,128)(2,1)}, bf16[1024,384]{0,1:T(8,128)(2,1)}, u32[]{:S(2)}, u32[]{:S(2)}) collective-permute-start(bf16[1024,384]{0,1:T(8,128)(2,1)} %bitcast.1), channel_id=1, source_target_pairs={{0,65},{1,64},{8,73},{9,72},{16,105},{17,104},{24,97},{25,96},{32,... | collective-permute-start | bytes 2359304 | tf_op jit(solution)/shard_map/ppermute | solution.py:47
  63.4 48.0 %collective-permute-start.10 = (bf16[1024,1024]{1,0:T(8,128)(2,1)}, bf16[1024,1024]{1,0:T(8,128)(2,1)}, u32[]{:S(2)}, u32[]{:S(2)}) collective-permute-start(bf16[1024,1024]{1,0:T(8,128)(2,1)} %bitcast.175), channel_id=1, source_target_pairs={{0,24},{8,16},{16,48},{24,56},{32,0},{40,8},{48,40},{56,32},{1,25}... | collective-permute-start | bytes 6291464 | tf_op jit(solution)/shard_map/ppermute | solution.py:47
  63.4 49.5 %collective-permute-start.11 = (bf16[1024,1024]{1,0:T(8,128)(2,1)}, bf16[1024,1024]{1,0:T(8,128)(2,1)}, u32[]{:S(2)}, u32[]{:S(2)}) collective-permute-start(bf16[1024,1024]{1,0:T(8,128)(2,1)} %bitcast.176), channel_id=1, source_target_pairs={{0,65},{1,64},{8,73},{9,72},{16,105},{17,104},{24,97},{25,96},{32,... | collective-permute-start | bytes 6291464 | tf_op jit(solution)/shard_map/ppermute | solution.py:47
  122.4 31.8 %all-to-all-start.2 = ((bf16[8,64,2048]{2,1,0:T(8,128)(2,1)}), bf16[8,64,2048]{2,1,0:T(8,128)(2,1)S(1)}, u32[]{:S(2)}, u32[]{:S(2)}) async-start(bf16[8,64,2048]{2,1,0:T(8,128)(2,1)} %bitcast.22), calls=%async_computation.2 | async-start | bytes 4194304 | tf_op jit(solution)/shard_map/all_to_all | solution.py:91
  126.5 24.2 %collective-permute-start.13 = (bf16[512,1024]{1,0:T(8,128)(2,1)}, bf16[512,1024]{1,0:T(8,128)(2,1)S(1)}, u32[]{:S(2)}, u32[]{:S(2)}) collective-permute-start(bf16[512,1024]{1,0:T(8,128)(2,1)} %param.17), channel_id=1, source_target_pairs={{0,24},{8,16},{16,48},{24,56},{32,0},{40,8},{48,40},{56,32},{1,25}... | collective-permute-start | bytes 3145736 | tf_op jit(solution)/shard_map/ppermute | solution.py:47
  127.1 27.0 %collective-permute-start.14 = (bf16[512,1024]{1,0:T(8,128)(2,1)}, bf16[512,1024]{1,0:T(8,128)(2,1)}, u32[]{:S(2)}, u32[]{:S(2)}) collective-permute-start(bf16[512,1024]{1,0:T(8,128)(2,1)} %param.17), channel_id=1, source_target_pairs={{0,65},{1,64},{8,73},{9,72},{16,105},{17,104},{24,97},{25,96},{32,... | collective-permute-start | bytes 3145736 | tf_op jit(solution)/shard_map/ppermute | solution.py:47
  157.3 23.8 %all-to-all-start.3 = ((bf16[8,64,2048]{2,1,0:T(8,128)(2,1)}), bf16[8,64,2048]{2,1,0:T(8,128)(2,1)S(1)}, u32[]{:S(2)}, u32[]{:S(2)}) async-start(bf16[8,64,2048]{2,1,0:T(8,128)(2,1)} %bitcast.29), calls=%async_computation.3 | async-start | bytes 4194304 | tf_op jit(solution)/shard_map/all_to_all | solution.py:91
  294.1 45.6 %all-to-all-start.6 = ((bf16[8,64,2048]{2,1,0:T(8,128)(2,1)}), bf16[8,64,2048]{2,1,0:T(8,128)(2,1)S(1)}, u32[]{:S(2)}, u32[]{:S(2)}) async-start(bf16[8,64,2048]{2,1,0:T(8,128)(2,1)} %bitcast.38), calls=%async_computation.6 | async-start | bytes 4194304 | tf_op jit(solution)/shard_map/all_to_all | solution.py:91
  313.9 25.8 %collective-permute-start.21 = (bf16[512,1024]{1,0:T(8,128)(2,1)}, bf16[512,1024]{1,0:T(8,128)(2,1)}, u32[]{:S(2)}, u32[]{:S(2)}) collective-permute-start(bf16[512,1024]{1,0:T(8,128)(2,1)} %get-tuple-element.168), channel_id=1, source_target_pairs={{0,65},{1,64},{8,73},{9,72},{16,105},{17,104},{24,97},{25,96},{32,... | collective-permute-start | bytes 3145736 | tf_op jit(solution)/shard_map/ppermute | solution.py:47
  345.7 33.0 %all-to-all-start.7 = ((bf16[8,64,2048]{2,1,0:T(8,128)(2,1)}), bf16[8,64,2048]{2,1,0:T(8,128)(2,1)}, u32[]{:S(2)}, u32[]{:S(2)}) async-start(bf16[8,64,2048]{2,1,0:T(8,128)(2,1)} %bitcast.44), calls=%async_computation.7 | async-start | bytes 4194304 | tf_op jit(solution)/shard_map/all_to_all | solution.py:91
  351.6 27.1 %collective-permute-start.25 = (bf16[512,1024]{1,0:T(8,128)(2,1)}, bf16[512,1024]{1,0:T(8,128)(2,1)S(1)}, u32[]{:S(2)}, u32[]{:S(2)}) collective-permute-start(bf16[512,1024]{1,0:T(8,128)(2,1)} %get-tuple-element.178), channel_id=1, source_target_pairs={{0,65},{1,64},{8,73},{9,72},{16,105},{17,104},{24,97},{25,96},{32,... | collective-permute-start | bytes 3145736 | tf_op jit(solution)/shard_map/ppermute | solution.py:47
  412.5 33.3 %collective-permute-start.28 = (bf16[512,1024]{1,0:T(8,128)(2,1)}, bf16[512,1024]{1,0:T(8,128)(2,1)S(1)}, u32[]{:S(2)}, u32[]{:S(2)}) collective-permute-start(bf16[512,1024]{1,0:T(8,128)(2,1)} %get-tuple-element.196), channel_id=1, source_target_pairs={{0,32},{8,40},{16,8},{24,0},{32,56},{40,48},{48,16},{56,24},{1,33}... | collective-permute-start | bytes 3145736 | tf_op jit(solution)/shard_map/ppermute | solution.py:47
  415.3 30.5 %collective-permute-start.29 = (bf16[512,1024]{1,0:T(8,128)(2,1)}, bf16[512,1024]{1,0:T(8,128)(2,1)}, u32[]{:S(2)}, u32[]{:S(2)}) collective-permute-start(bf16[512,1024]{1,0:T(8,128)(2,1)} %get-tuple-element.197), channel_id=1, source_target_pairs={{0,65},{1,64},{8,73},{9,72},{16,105},{17,104},{24,97},{25,96},{32,... | collective-permute-start | bytes 3145736 | tf_op jit(solution)/shard_map/ppermute | solution.py:47
  416.2 25.3 %collective-permute-start.30 = (bf16[128,1024]{1,0:T(8,128)(2,1)}, bf16[128,1024]{1,0:T(8,128)(2,1)}, u32[]{:S(2)}, u32[]{:S(2)}) collective-permute-start(bf16[128,1024]{1,0:T(8,128)(2,1)} %get-tuple-element.198), channel_id=1, source_target_pairs={{0,32},{8,40},{16,8},{24,0},{32,56},{40,48},{48,16},{56,24},{1,33}... | collective-permute-start | bytes 786440 | tf_op jit(solution)/shard_map/ppermute | solution.py:47
  416.5 29.3 %collective-permute-start.31 = (bf16[128,1024]{1,0:T(8,128)(2,1)}, bf16[128,1024]{1,0:T(8,128)(2,1)}, u32[]{:S(2)}, u32[]{:S(2)}) collective-permute-start(bf16[128,1024]{1,0:T(8,128)(2,1)} %get-tuple-element.199), channel_id=1, source_target_pairs={{0,65},{1,64},{8,73},{9,72},{16,105},{17,104},{24,97},{25,96},{32,... | collective-permute-start | bytes 786440 | tf_op jit(solution)/shard_map/ppermute | solution.py:47
  420.4 25.4 %collective-permute-start.32 = (bf16[256,1024]{1,0:T(8,128)(2,1)}, bf16[256,1024]{1,0:T(8,128)(2,1)S(1)}, u32[]{:S(2)}, u32[]{:S(2)}) collective-permute-start(bf16[256,1024]{1,0:T(8,128)(2,1)} %add_convert_fusion.12), channel_id=1, source_target_pairs={{0,64},{64,0},{1,65},{65,1},{2,66},{66,2},{3,67},{67,3},{4,68},{68... | collective-permute-start | bytes 1572872 | tf_op jit(solution)/shard_map/ppermute | solution.py:47
  473.4 38.1 %all-to-all-start.9 = ((bf16[8,64,2048]{2,1,0:T(8,128)(2,1)}), bf16[8,64,2048]{2,1,0:T(8,128)(2,1)S(1)}, u32[]{:S(2)}, u32[]{:S(2)}) async-start(bf16[8,64,2048]{2,1,0:T(8,128)(2,1)} %bitcast.68), calls=%async_computation.9 | async-start | bytes 4194304 | tf_op jit(solution)/shard_map/all_to_all | solution.py:91
  482.6 28.8 %collective-permute-start.37 = (bf16[1024,384]{1,0:T(8,128)(2,1)}, bf16[1024,384]{1,0:T(8,128)(2,1)}, u32[]{:S(2)}, u32[]{:S(2)}) collective-permute-start(bf16[1024,384]{1,0:T(8,128)(2,1)} %get-tuple-element.215), channel_id=1, source_target_pairs={{0,32},{8,40},{16,8},{24,0},{32,56},{40,48},{48,16},{56,24},{1,33}... | collective-permute-start | bytes 2359304 | tf_op jit(solution)/shard_map/ppermute | solution.py:47
  484.1 27.3 %collective-permute-start.38 = (bf16[1024,384]{1,0:T(8,128)(2,1)}, bf16[1024,384]{1,0:T(8,128)(2,1)}, u32[]{:S(2)}, u32[]{:S(2)}) collective-permute-start(bf16[1024,384]{1,0:T(8,128)(2,1)} %get-tuple-element.216), channel_id=1, source_target_pairs={{0,65},{1,64},{8,73},{9,72},{16,105},{17,104},{24,97},{25,96},{32,... | collective-permute-start | bytes 2359304 | tf_op jit(solution)/shard_map/ppermute | solution.py:47
  484.9 26.5 %collective-permute-start.39 = (bf16[256,1024]{1,0:T(8,128)(2,1)S(1)}, bf16[256,1024]{1,0:T(8,128)(2,1)}, u32[]{:S(2)}, u32[]{:S(2)}) collective-permute-start(bf16[256,1024]{1,0:T(8,128)(2,1)S(1)} %copy-done.30), channel_id=1, source_target_pairs={{0,64},{64,0},{1,65},{65,1},{2,66},{66,2},{3,67},{67,3},{4,68},{68... | collective-permute-start | bytes 1572872 | tf_op jit(solution)/shard_map/ppermute | solution.py:47
  485.2 26.3 %collective-permute-start.40 = (bf16[256,1024]{1,0:T(8,128)(2,1)}, bf16[256,1024]{1,0:T(8,128)(2,1)}, u32[]{:S(2)}, u32[]{:S(2)}) collective-permute-start(bf16[256,1024]{1,0:T(8,128)(2,1)} %add_convert_fusion.10), channel_id=1, source_target_pairs={{0,64},{64,0},{1,65},{65,1},{2,66},{66,2},{3,67},{67,3},{4,68},{68... | collective-permute-start | bytes 1572872 | tf_op jit(solution)/shard_map/ppermute | solution.py:47
  486.5 24.9 %collective-permute-start.41 = (bf16[64,1024]{1,0:T(8,128)(2,1)S(1)}, bf16[64,1024]{1,0:T(8,128)(2,1)}, u32[]{:S(2)}, u32[]{:S(2)}) collective-permute-start(bf16[64,1024]{1,0:T(8,128)(2,1)S(1)} %add_convert_fusion.18), channel_id=1, source_target_pairs={{0,64},{64,0},{1,65},{65,1},{2,66},{66,2},{3,67},{67,3},{4,68},{68... | collective-permute-start | bytes 393224 | tf_op jit(solution)/shard_map/ppermute | solution.py:47
  (125 other events, 1168.9 us)
